TPU v7x, 256 devices: a whole 4x4x8 slice. The times are simulated.
256 devices in a mesh: row: 32 (over z_hi, x, core), col: 8 (over y, z_lo).
Axes of the slice: x: 4, y: 4, z: 8 (z_hi: 4, z_lo: 2; z = z_hi * 2 + z_lo), core: 2. Of those that a mesh axis runs over, the one named last changes fastest.
Arguments:
- pair_valence: int32 [4096], P(('row', 'col')), may hold values from 0 to 63
- pair_conduction: int32 [4096], P(('row', 'col')), may hold values from 0 to 3071
- elements: bfloat16 [4096, 12288], P(('row', 'col')), may hold values from -0.09375 to 0.09375
- valence_energy: float32 [64], replicated, may hold values from -12 to -0.5
- conduction_energy: float32 [3072], replicated, may hold values from 0.5 to 25
- coulomb_sqrt: float32 [12288], replicated, may hold values from 0.3 to 3
Outputs:
- chi_sym: float32 [12288, 12288], P('row', 'col')
All inputs are finite; a program needn't handle non-finite values.
Results may differ from a plain program's by a relative error of at most 0.0025.
Values may be sent and summed in bfloat16 or wider, within the bound.
A program may use at most 128 MiB of HBM per device.

v0:
```python
import jax
import jax.numpy as jnp
from jax import lax
from jax.sharding import PartitionSpec as P


def lookup(indices, table):
    slots = lax.broadcasted_iota(jnp.int32, (indices.shape[0], table.shape[0]), 1)
    picked = jnp.where(indices[:, None] == slots, table[None, :], 0.0)
    return jnp.sum(picked, axis=1)


def contract(left, right):
    return lax.dot_general(
        left, right, (((0,), (0,)), ((), ())), preferred_element_type=jnp.float32
    )


def per_device(
    pair_valence, pair_conduction, elements, valence_energy, conduction_energy, coulomb_sqrt
):
    n_row = lax.axis_size("row")
    n_col = lax.axis_size("col")
    width = elements.shape[1]
    row_block = width // n_row
    col_block = width // n_col
    lower = lookup(pair_valence, valence_energy)
    upper = lookup(pair_conduction, conduction_energy)
    weight = 4.0 / (lower - upper)
    scaled = (weight[:, None] * elements.astype(jnp.float32)).astype(jnp.bfloat16)
    grouped = lax.all_gather(scaled, "col", axis=0, tiled=True)
    row_panel = lax.all_to_all(grouped, "row", split_axis=1, concat_axis=0, tiled=True)
    own_pairs = lax.all_to_all(elements, "col", split_axis=1, concat_axis=0, tiled=True)
    chi_zero = contract(row_panel, lax.all_gather(own_pairs, "row", axis=0, tiled=True))
    row_scale = lax.dynamic_slice_in_dim(
        coulomb_sqrt, lax.axis_index("row") * row_block, row_block, 0
    )
    col_scale = lax.dynamic_slice_in_dim(
        coulomb_sqrt, lax.axis_index("col") * col_block, col_block, 0
    )
    return row_scale[:, None] * chi_zero * col_scale[None, :]


def solution(mesh):
    placed = (P(("row", "col")), P(("row", "col")), P(("row", "col"), None), P(), P(), P())
    return jax.shard_map(
        per_device, mesh=mesh, in_specs=placed, out_specs=P("row", "col"), check_vma=False
    )
```

profile of v0, /device:TPU:3, one launch (start us, length us, event | category | flops | bytes accessed | tf_op | source)
XLA Modules:
  0.0 261.3 jit_solution(13951718351481736634)
XLA Ops:
  6.5 0.0 all-gather.3.cloned.1.call-start
  6.5 0.9 select_reduce_fusion.1
  7.4 0.9 select_reduce_fusion
  8.3 1.9 multiply_convert_fusion
  10.2 0.0 all-gather.3.cloned.1.call-update
  10.2 0.0 all-gather.5.cloned.1.call-start
  10.3 1.0 copy.19
  11.3 13.2 %all_to_all.38 = bf16[16,8,1536]{2,0,1:T(8,128)(2,1)} all-to-all(bf16[16,8,1536]{2,0,1:T(8,128)(2,1)S(1)} %bitcast.16), channel_id=1, replica_groups=mesh['row'=32,'col'=8] {'col'}, dimensions={1} | all-to-all | bytes 786432 | tf_op jit(solution)/shard_map/all_to_all | solution.py:33
  24.5 0.0 all-gather.5.cloned.1.call-update
  24.5 62.6 %all-gather.3.cloned.1.call-done = bf16[128,12288]{1,0:T(8,128)(2,1)} async-done(((bf16[16,12288]{1,0:T(8,128)(2,1)}), bf16[128,12288]{1,0:T(8,128)(2,1)}) %all-gather.3.cloned.1.call-update) | async-done | bytes 3145744 | tf_op jit(solution)/shard_map/all_gather | solution.py:31
  87.2 4.7 %copy.14 = bf16[128,12288]{0,1:T(8,128)(2,1)} copy(bf16[128,12288]{1,0:T(8,128)(2,1)} %all-gather.3.cloned.1.call-done) | data formatting | bytes 6291456 | tf_op jit(solution)/shard_map/all_gather | solution.py:31
  91.9 9.8 %all-to-all-start = ((bf16[128,32,384]{0,2,1:T(8,128)(2,1)}), bf16[128,32,384]{0,2,1:T(8,128)(2,1)S(1)}, u32[]{:S(2)}, u32[]{:S(2)}) async-start(bf16[128,32,384]{0,2,1:T(8,128)(2,1)} %bitcast.13), calls=%async_computation | async-start | bytes 6291456 | tf_op jit(solution)/shard_map/all_to_all | solution.py:32
  101.7 0.8 dynamic_slice.6
  102.5 0.8 dynamic_slice.7
  103.2 83.5 %all-to-all-done = bf16[128,32,384]{0,2,1:T(8,128)(2,1)S(1)} async-done(((bf16[128,32,384]{0,2,1:T(8,128)(2,1)}), bf16[128,32,384]{0,2,1:T(8,128)(2,1)S(1)}, u32[]{:S(2)}, u32[]{:S(2)}) %all-to-all-start) | async-done | bytes 3145760 | tf_op jit(solution)/shard_map/all_to_all | solution.py:32
  186.8 2.9 %copy.15 = bf16[32,128,384]{2,1,0:T(8,128)(2,1)} copy(bf16[32,128,384]{1,2,0:T(8,128)(2,1)S(1)} %bitcast.12) | data formatting | bytes 6291456 | tf_op jit(solution)/shard_map/all_to_all | solution.py:32
  189.6 54.9 %all-gather.5.cloned.1.call-done = bf16[4096,1536]{1,0:T(8,128)(2,1)} async-done(((bf16[128,1536]{1,0:T(8,128)(2,1)}), bf16[4096,1536]{1,0:T(8,128)(2,1)}) %all-gather.5.cloned.1.call-update) | async-done | bytes 12582928 | tf_op jit(solution)/shard_map/all_gather | solution.py:34
  244.5 10.0 %fusion = f32[384,1536]{1,0:T(8,128)} fusion(bf16[4096,384]{1,0:T(8,128)(2,1)} %bitcast.14, bf16[4096,1536]{1,0:T(8,128)(2,1)} %all-gather.5.cloned.1.call-done, f32[1536]{0:T(1024)S(1)} %dynamic_slice.7, f32[384]{0:T(512)S(1)} %dynamic_slice.6), kind=kOutput, calls=%fused_computation.1 | convolution fusion | flops 4833017856 | bytes 18095616 | tf_op jit(solution)/shard_map/dot_general | solution.py:14
  (1 shorter events, 0.0 us)
Async XLA Ops:
  6.5 80.6 %all-gather.3.cloned.1.call-start = ((), (), s32[]{:S(2)}) async-start(), calls=%async_computation.2 | async-start | bytes 3538944 | tf_op jit(solution)/shard_map/all_gather | solution.py:31
  10.2 234.2 %all-gather.5.cloned.1.call-start = ((), (), s32[]{:S(2)}) async-start(), calls=%async_computation.3 | async-start | bytes 12976128 | tf_op jit(solution)/shard_map/all_gather | solution.py:34
  91.9 94.9 %all-to-all-start = ((bf16[128,32,384]{0,2,1:T(8,128)(2,1)}), bf16[128,32,384]{0,2,1:T(8,128)(2,1)S(1)}, u32[]{:S(2)}, u32[]{:S(2)}) async-start(bf16[128,32,384]{0,2,1:T(8,128)(2,1)} %bitcast.13), calls=%async_computation | async-start | bytes 6291456 | tf_op jit(solution)/shard_map/all_to_all | solution.py:32
Sparse Core Ops, SparseCore 0:
  10.3 76.7 all-gather.2
  89.7 154.7 all-gather.4
where the time goes:
time: 262 us; the launch traced here: 261 us
  waiting for transfers between devices  201 us (77%)
  between operations  13.4 us (5%)
  blocking collectives  13.2 us (5%)
  local copies, waits for them, and re-layouts  10.1 us (4%)
  matrix products  10 us (4%)
  starting transfers between devices  9.81 us (4%)
  other arithmetic  3.66 us (1%)
    all_to_all x1, waiting for transfers between devices, per_device(): lax.all_to_all(grouped, 'row', split_axis=1, concat_axis=0, tiled=True)  83.5 us
    all_gather x1, waiting for transfers between devices, per_device(): grouped = lax.all_gather(scaled, 'col', axis=0, tiled=True)  62.6 us
    all_gather x1, waiting for transfers between devices, per_device(): lax.all_gather(own_pairs, 'row', axis=0, tiled=True)  54.9 us
    all_to_all x1, blocking collectives, per_device(): lax.all_to_all(elements, 'col', split_axis=1, concat_axis=0, tiled=True)  13.2 us
    dot_general x1, matrix products, contract(): lax.dot_general(left, right, (((0,), (0,)), ((), ())), preferred_element_...  10 us
    all_to_all x1, starting transfers between devices, per_device(): lax.all_to_all(grouped, 'row', split_axis=1, concat_axis=0, tiled=True)  9.77 us
  transfers between devices with their start and end apart: 3, of which 3 were waited for; matrix products, arithmetic and copies ran while one was open for 4% of the time, Pallas kernels for 0%

commit v1 on v0

v1 whole, which is shorter than its diff:
```python
import functools

import jax
import jax.numpy as jnp
from jax import lax
from jax.experimental import pallas as pl
from jax.experimental.pallas import tpu as pltpu
from jax.sharding import PartitionSpec as P

MESH = pl.DeviceIdType.MESH
F32, BF16 = jnp.float32, jnp.bfloat16

PAIRS_HERE = 16
WIDE = 1536
HALF = WIDE // 2
QUARTER = WIDE // 4
CHUNKS = ((0, 256), (256, 256), (512, 256), (768, 256), (1024, 256), (1280, 256))
GROUPS = ((0, 512), (512, 512), (1024, 512))


def kernel(
    val_ref, cond_ref, e_ref, ve_ref, ce_ref, cs_ref, out_ref,
    es, a_in, at, bp, c_give, c_keep, c_got, p_give, p_got, out_v,
    a2a_s, a2a_r, ag_s, ag_r, bg_s, bg_r, c_s, c_r, p_s, p_r, o_s,
):
    row, col = lax.axis_index("row"), lax.axis_index("col")
    core, x, zh = row % 2, (row // 2) % 4, row // 8
    y, zl = col // 2, col % 2
    xh, xl = x // 2, x % 2

    def device(x_, y_, zh_, zl_, core_):
        return ((zh_ * 4 + x_) * 2 + core_, y_ * 2 + zl_)

    pair_peers = []
    for mirror in (0, 1):
        for dz in range(4):
            if mirror or dz:
                x_ = 3 - x if mirror else x
                pair_peers.append((x_, (zh + dz) % 4))
    block_peers = [((y + d // 2) % 4, (zl + d % 2) % 2) for d in range(1, 8)]
    other_core = device(x, y, zh, zl, 1 - core)
    neighbour = device(x + 1 - 2 * xl, y, zh, zl, core)
    mirror_dev = device(3 - x, y, zh, zl, core)
    z_up = device(x, y, (zh + 1) % 4, zl, core)
    z_down = device(x, y, (zh + 3) % 4, zl, core)
    z_mate = device(x, y, zh, 1 - zl, core)
    y_up = device(x, (y + 1) % 4, zh, zl, core)
    y_down = device(x, (y + 3) % 4, zh, zl, core)

    barrier = pltpu.get_barrier_semaphore()
    everyone = [device(x_, y, zh_, zl, core) for x_, zh_ in pair_peers]
    everyone += [device(x, y_, zh, zl_, core) for y_, zl_ in block_peers]
    everyone += [other_core, neighbour]
    for peer in everyone:
        pl.semaphore_signal(barrier, inc=1, device_id=peer, device_id_type=MESH)

    sent = []

    def send(src, dst, send_sem, recv_sem, peer):
        copy = pltpu.make_async_remote_copy(
            src_ref=src, dst_ref=dst, send_sem=send_sem, recv_sem=recv_sem,
            device_id=peer, device_id_type=MESH,
        )
        copy.start()
        return copy

    def pick(idx_ref, table):
        slots = lax.broadcasted_iota(jnp.int32, table.shape, 0) * table.shape[1]
        slots += lax.broadcasted_iota(jnp.int32, table.shape, 1)
        rows = [
            jnp.sum(jnp.where(slots == idx_ref[i], table, 0.0), axis=0, keepdims=True)
            for i in range(PAIRS_HERE)
        ]
        return jnp.sum(jnp.concatenate(rows, axis=0), axis=1, keepdims=True)

    weight = 4.0 / (pick(val_ref, ve_ref[...]) - pick(cond_ref, ce_ref[...]))
    for j in range(0, e_ref.shape[1], HALF):
        part = e_ref[:, j : j + HALF].astype(F32)
        es[:, j : j + HALF] = (weight * part).astype(BF16)

    pl.semaphore_wait(barrier, len(everyone))

    spot = xh * 4 + zh
    deep = pl.ds(spot * PAIRS_HERE, PAIRS_HERE)

    def send_b(g):
        start, width = GROUPS[g]
        copies = []
        for y_, zl_ in block_peers:
            c_ = y_ * 2 + zl_
            cols = pl.ds(pl.multiple_of(c_ * WIDE + start, 256), width)
            copies.append(
                send(
                    e_ref.at[:, cols],
                    bp.at[col, spot, :, pl.ds(start, width)],
                    a2a_s.at[2 + g], a2a_r.at[2 + g],
                    device(x, y_, zh, zl_, core),
                )
            )
        cols = pl.ds(pl.multiple_of(col * WIDE + start, 256), width)
        bp[col, spot, :, pl.ds(start, width)] = e_ref[:, cols]

    def wait_b(g):
        start, width = GROUPS[g]
        ref = bp.at[pl.ds(0, 7), 0, :, pl.ds(start, width)]
        pltpu.make_async_copy(ref, ref, a2a_r.at[2 + g]).wait()

    def send_a(h):
        def cols_of(x_, zh_):
            part = 1 - x_ % 2 if h == 0 else x_ % 2
            return pl.ds(pl.multiple_of((zh_ * 2 + x_ // 2) * WIDE + part * HALF, 256), HALF)

        for x_, zh_ in pair_peers:
            send(
                es.at[:, cols_of(x_, zh_)], a_in.at[h, deep, :],
                a2a_s.at[h], a2a_r.at[h], device(x_, y, zh_, zl, core),
            )
        a_in[h, deep, :] = es[:, cols_of(x, zh)]

    def wait_a(h):
        ref = a_in.at[h, pl.ds(0, 7 * PAIRS_HERE), :]
        pltpu.make_async_copy(ref, ref, a2a_r.at[h]).wait()

    mate = y * 2 + 1 - zl
    up2, down2 = (y + 1) % 4 * 2, (y + 3) % 4 * 2

    def ag(h, n, slot, peer, rows=None):
        ref = at.at[h, slot] if rows is None else at.at[h, slot, pl.ds(*rows)]
        copy = send(ref, ref, ag_s.at[h, n], ag_r.at[h, n], peer)
        sent.append(copy)
        return copy

    def a_first(h):
        wait_a(h)
        at[h, col] = a_in[h].T
        return [ag(h, 0, col, z_mate), ag(h, 1, col, y_up), ag(h, 2, col, y_down)]

    def a_second(h, first):
        first[0].wait_recv()
        return [ag(h, 3, mate, y_up), ag(h, 4, mate, y_down)]

    lo, hi = (0, QUARTER), (QUARTER, QUARTER)

    def a_third(h, first):
        first[1].wait_recv()
        one = ag(h, 5, down2 + zl, y_up, lo)
        first[2].wait_recv()
        return [one, ag(h, 6, up2 + zl, y_down, hi)]

    def a_fourth(h, second):
        second[0].wait_recv()
        one = ag(h, 7, down2 + 1 - zl, y_up, lo)
        second[1].wait_recv()
        return [one, ag(h, 8, up2 + 1 - zl, y_down, hi)]

    def a_last(copies):
        for copy in copies:
            copy.wait_recv()

    s_up, s_down, s_far = (xh * 4 + (zh + d) % 4 for d in (1, 3, 2))

    def bg(j, n, s, peer, rows=None):
        start, width = CHUNKS[j]
        rows = pl.ds(0, 8) if rows is None else pl.ds(*rows)
        ref = bp.at[rows, s, :, pl.ds(start, width)]
        copy = send(ref, ref, bg_s.at[j, n], bg_r.at[j, n], peer)
        sent.append(copy)
        return copy

    chunks = [dict() for _ in CHUNKS]

    def b_first(j):
        d = chunks[j]
        d["up"] = bg(j, 0, spot, z_up)
        d["down"] = bg(j, 1, spot, z_down)
        d["m0"] = bg(j, 2, spot, mirror_dev)

    def b_second(j):
        d = chunks[j]
        d["up"].wait_recv()
        d["far0"] = bg(j, 3, s_down, z_up, (0, 4))
        d["m1"] = bg(j, 4, s_down, mirror_dev)
        d["down"].wait_recv()
        d["far1"] = bg(j, 5, s_up, z_down, (4, 4))
        d["m2"] = bg(j, 6, s_up, mirror_dev)

    def b_third(j):
        d = chunks[j]
        d["far0"].wait_recv()
        d["far1"].wait_recv()
        d["m3"] = bg(j, 7, s_far, mirror_dev)

    def b_last(j):
        for n in range(4):
            chunks[j][f"m{n}"].wait_recv()

    def product(j, h, q):
        start, width = CHUNKS[j]
        rows = pl.ds(pl.multiple_of(q * QUARTER, QUARTER), QUARTER)
        left = jnp.concatenate([at[h, n, rows, :] for n in range(8)], axis=1)
        right = bp[:, :, :, start : start + width].reshape(1024, width)
        return jnp.dot(left, right, preferred_element_type=F32)

    def multiply(j, h):
        start, width = CHUNKS[j]
        cols = pl.ds(start, width)
        c_give[h, :, cols] = product(j, h, 1 - core)
        copy = send(
            c_give.at[h, :, cols], c_got.at[h, :, cols], c_s.at[j, h], c_r.at[j, h], other_core
        )
        sent.append(copy)
        chunks[j][f"c{h}"] = copy
        c_keep[h, :, cols] = product(j, h, core)

    def give(j):
        start, width = CHUNKS[j]
        cols = pl.ds(start, width)
        chunks[j]["c0"].wait_recv()
        p_give[:, cols] = (c_keep[0, :, cols] + c_got[0, :, cols]).astype(BF16)
        copy = send(p_give.at[:, cols], p_got.at[:, cols], p_s.at[j], p_r.at[j], neighbour)
        sent.append(copy)
        chunks[j]["p"] = copy

    eye = lax.broadcasted_iota(jnp.int32, (128, 128), 0) == lax.broadcasted_iota(
        jnp.int32, (128, 128), 1
    )
    row_scale = []
    for i in range(QUARTER // 128):
        line = cs_ref[:, pl.ds(pl.multiple_of(row * QUARTER + i * 128, 128), 128)]
        row_scale.append(jnp.sum(jnp.where(eye, line, 0.0), axis=1, keepdims=True))
    row_scale = jnp.concatenate(row_scale, axis=0)

    def finish(j):
        start, width = CHUNKS[j]
        cols = pl.ds(start, width)
        chunks[j]["c1"].wait_recv()
        chunks[j]["p"].wait_recv()
        total = c_keep[1, :, cols] + c_got[1, :, cols] + p_got[:, cols].astype(F32)
        col_scale = cs_ref[:, pl.ds(pl.multiple_of(col * WIDE + start, 128), width)]
        out_v[:, cols] = row_scale * total * col_scale
        copy = pltpu.make_async_copy(out_v.at[:, cols], out_ref.at[:, cols], o_s.at[j])
        copy.start()
        return copy

    outs = []
    send_b(0)
    send_a(0)
    send_b(1)
    send_a(1)
    send_b(2)
    wait_b(0)
    b_first(0)
    b_first(1)
    t1 = a_first(0)
    wait_b(1)
    b_second(0)
    b_first(2)
    t2 = a_second(0, t1)
    b_second(1)
    b_first(3)
    t3 = a_third(0, t1)
    u1 = a_first(1)
    b_third(0)
    t4 = a_fourth(0, t2)
    wait_b(2)
    b_second(2)
    b_third(1)
    b_first(4)
    u2 = a_second(1, u1)
    b_last(0)
    a_last(t3 + t4)
    multiply(0, 0)
    b_second(3)
    b_third(2)
    b_first(5)
    give(0)
    u3 = a_third(1, u1)
    b_last(1)
    multiply(1, 0)
    give(1)
    b_second(4)
    b_third(3)
    u4 = a_fourth(1, u2)
    b_last(2)
    multiply(2, 0)
    give(2)
    b_second(5)
    b_third(4)
    b_last(3)
    multiply(3, 0)
    give(3)
    a_last(u3 + u4)
    multiply(0, 1)
    multiply(1, 1)
    b_third(5)
    b_last(4)
    multiply(4, 0)
    give(4)
    multiply(2, 1)
    outs.append(finish(0))
    outs.append(finish(1))
    b_last(5)
    multiply(5, 0)
    give(5)
    multiply(3, 1)
    multiply(4, 1)
    multiply(5, 1)
    outs += [finish(j) for j in range(2, 6)]

    for copy in outs:
        copy.wait()
    for copy in sent:
        copy.wait_send()
    for h in range(2):
        ref = a_in.at[h, pl.ds(0, 7 * PAIRS_HERE), :]
        pltpu.make_async_copy(ref, ref, a2a_s.at[h]).wait()
    for g, (start, width) in enumerate(GROUPS):
        ref = bp.at[pl.ds(0, 7), 0, :, pl.ds(start, width)]
        pltpu.make_async_copy(ref, ref, a2a_s.at[2 + g]).wait()


def per_device(
    pair_valence, pair_conduction, elements, valence_energy, conduction_energy, coulomb_sqrt
):
    n = len(CHUNKS)
    smem = pl.BlockSpec(memory_space=pltpu.SMEM)
    vmem = pl.BlockSpec(memory_space=pltpu.VMEM)
    dma = pltpu.SemaphoreType.DMA
    return pl.pallas_call(
        kernel,
        out_shape=jax.ShapeDtypeStruct((QUARTER, WIDE), F32),
        in_specs=[smem, smem, vmem, vmem, vmem, vmem],
        out_specs=pl.BlockSpec(memory_space=pl.ANY),
        scratch_shapes=[
            pltpu.VMEM(elements.shape, BF16),
            pltpu.VMEM((2, 128, HALF), BF16),
            pltpu.VMEM((2, 8, HALF, 128), BF16),
            pltpu.VMEM((8, 8, PAIRS_HERE, WIDE), BF16),
            pltpu.VMEM((2, QUARTER, WIDE), F32),
            pltpu.VMEM((2, QUARTER, WIDE), F32),
            pltpu.VMEM((2, QUARTER, WIDE), F32),
            pltpu.VMEM((QUARTER, WIDE), BF16),
            pltpu.VMEM((QUARTER, WIDE), BF16),
            pltpu.VMEM((QUARTER, WIDE), F32),
            dma((5,)), dma((5,)),
            dma((2, 9)), dma((2, 9)),
            dma((n, 8)), dma((n, 8)),
            dma((n, 2)), dma((n, 2)),
            dma((n,)), dma((n,)),
            dma((n,)),
        ],
        compiler_params=pltpu.CompilerParams(
            collective_id=0, has_side_effects=True, vmem_limit_bytes=48 * 2**20
        ),
        cost_estimate=pl.CostEstimate(
            flops=2 * 1024 * WIDE * WIDE, bytes_accessed=3 * 2**20, transcendentals=0
        ),
    )(
        pair_valence,
        pair_conduction,
        elements,
        valence_energy.reshape(1, -1),
        conduction_energy.reshape(-1, 128),
        coulomb_sqrt.reshape(1, -1),
    )


def solution(mesh):
    placed = (P(("row", "col")), P(("row", "col")), P(("row", "col"), None), P(), P(), P())
    return jax.shard_map(
        per_device, mesh=mesh, in_specs=placed, out_specs=P("row", "col"), check_vma=False
    )
```

time: 262 us -> 89.2 us (0.34)
  waiting for transfers between devices: 201 us -> 0 us
  Pallas kernels: 0 us -> 82.5 us
  between operations: 13.4 us -> 0.02 us
  blocking collectives: 13.2 us -> 0 us
  matrix products: 10 us -> 0 us
  starting transfers between devices: 9.81 us -> 0 us
  local copies, waits for them, and re-layouts: 10.1 us -> 5.87 us
  other arithmetic: 3.66 us -> 0 us
    all_gather x2 -> x0, waiting for transfers between devices: 117 us -> none  [the longest x1 62.6 us: per_device(): grouped = lax.all_gather(scaled, 'col', axis=0, tiled=True)]
    all_to_all x1 -> x0, waiting for transfers between devices: 83.5 us -> none  [per_device(): lax.all_to_all(grouped, 'row', split_axis=1, concat_axis=0, tiled=True)]
    pallas_call x0 -> x1, Pallas kernels: none -> 82.5 us  [per_device(): pl.pallas_call(kernel, out_shape=jax.ShapeDtypeStruct((QUARTER, WIDE), F3...]
    all_to_all x1 -> x0, blocking collectives: 13.2 us -> none  [per_device(): lax.all_to_all(elements, 'col', split_axis=1, concat_axis=0, tiled=True)]
    dot_general x1 -> x0, matrix products: 10 us -> none  [contract(): lax.dot_general(left, right, (((0,), (0,)), ((), ())), preferred_element_...]
    all_to_all x1 -> x0, starting transfers between devices: 9.77 us -> none  [per_device(): lax.all_to_all(grouped, 'row', split_axis=1, concat_axis=0, tiled=True)]
    unnamed x0 -> x13, local copies, waits for them, and re-layouts: none -> 5.87 us
    all_gather x1 -> x0, local copies, waits for them, and re-layouts: 4.71 us -> none  [per_device(): grouped = lax.all_gather(scaled, 'col', axis=0, tiled=True)]
  transfers between devices with their start and end apart: 3 -> 0, of which waited for: 3 -> 0; matrix products, arithmetic and copies ran while one was open for 4% -> 0% of each run, Pallas kernels for 0% -> 0%
where the time goes in v1:
time: 89.2 us; the launch traced here: 88.4 us
  Pallas kernels  82.5 us (92%)
  local copies, waits for them, and re-layouts  5.87 us (7%)
    pallas_call x1, Pallas kernels, per_device(): pl.pallas_call(kernel, out_shape=jax.ShapeDtypeStruct((QUARTER, WIDE), F3...  82.5 us
    unnamed x13, local copies, waits for them, and re-layouts  5.87 us

profile of v1, /device:TPU:3, one launch (start us, length us, event | category | flops | bytes accessed | tf_op | source)
XLA Modules:
  0.0 88.4 jit_solution(1291395516149891690)
XLA Ops:
  0.0 0.0 copy-start
  0.0 1.0 %copy-done = bf16[16,12288]{1,0:T(8,128)(2,1)S(1)} copy-done((bf16[16,12288]{1,0:T(8,128)(2,1)S(1)}, bf16[16,12288]{1,0:T(8,128)(2,1)}, u32[]{:S(2)}) %copy-start) | copy-done | bytes 393240
  1.0 0.0 copy-start.1
  1.0 0.8 copy-done.1
  1.8 0.0 copy-start.2
  1.8 0.7 copy-done.2
  2.5 0.0 copy-start.3
  2.5 0.7 copy-done.3
  3.2 0.0 copy-start.4
  3.2 0.7 copy-done.4
  3.8 0.0 copy-start.5
  3.8 0.7 copy-done.5
  4.5 82.5 %shard_map.64 = f32[384,1536]{1,0:T(8,128)S(1)} custom-call(s32[16]{0:T(128)S(1)} %copy-done.3, s32[16]{0:T(128)S(1)} %copy-done.4, bf16[16,12288]{1,0:T(8,128)(2,1)S(1)} %copy-done, f32[1,64]{1,0:T(1,128)S(1)} %bitcast.5, f32[24,128]{1,0:T(8,128)S(1)} %bitcast.4, f32[1,12288]{1,0:T(1,128)S(1)} %bitcast.3), custom_call_target="tpu_custom_call" | custom-call | flops 4831838208 | bytes 3145728 | tf_op jit(solution)/shard_map/pallas_call | solution.py:329
  87.0 1.4 %copy.8 = f32[384,1536]{1,0:T(8,128)} copy(f32[384,1536]{1,0:T(8,128)S(1)} %shard_map.64) | data formatting | bytes 4718592
Async XLA Ops:
  0.0 1.0 %copy-start = (bf16[16,12288]{1,0:T(8,128)(2,1)S(1)}, bf16[16,12288]{1,0:T(8,128)(2,1)}, u32[]{:S(2)}) copy-start(bf16[16,12288]{1,0:T(8,128)(2,1)} %e_ref.1) | copy-start | bytes 1179652
  1.0 0.8 copy-start.1
  1.8 0.7 copy-start.2
  2.5 0.7 copy-start.3
  3.2 0.7 copy-start.4
  3.8 0.7 copy-start.5

commit v2 on v1

v2 whole, which is shorter than its diff:
```python
import jax
import jax.numpy as jnp
from jax import lax
from jax.experimental import pallas as pl
from jax.experimental.pallas import tpu as pltpu
from jax.sharding import PartitionSpec as P

MESH = pl.DeviceIdType.MESH
F32, BF16 = jnp.float32, jnp.bfloat16

PAIRS_HERE = 16
WIDE = 1536
HALF = WIDE // 2
QUARTER = WIDE // 4
CHUNK = 256
CHUNKS = WIDE // CHUNK
GROUP = 2


def kernel(
    val_hbm, cond_hbm, e_hbm, ve_hbm, ce_hbm, cs_hbm, out_ref,
    val_ref, cond_ref, e_ref, ve_ref, ce_ref, cs_ref, in_s,
    es, a_in, at, bp, xs, c_own, c_got, p_give, p_got,
    a2a_s, a2a_r, ag_s, ag_r, bg_s, bg_r, c_s, c_r, p_s, p_r,
):
    loads = [
        pltpu.make_async_copy(far, near, in_s.at[i])
        for i, (far, near) in enumerate(
            (
                (e_hbm, e_ref), (val_hbm, val_ref), (cond_hbm, cond_ref),
                (ve_hbm, ve_ref), (ce_hbm, ce_ref), (cs_hbm, cs_ref),
            )
        )
    ]
    for load in loads:
        load.start()

    row, col = lax.axis_index("row"), lax.axis_index("col")
    core, x, zh = row % 2, (row // 2) % 4, row // 8
    y, zl = col // 2, col % 2
    xh, xl, z = x // 2, x % 2, zh * 2 + zl
    toward = 1 - 2 * zl

    def device(x_, y_, z_, core_):
        return ((z_ // 2 * 4 + x_) * 2 + core_, y_ * 2 + z_ % 2)

    def z_at(step):
        return (z + step + 8) % 8

    mirror = 3 - x
    mirror_dev = device(mirror, y, z, core)
    other_core = device(x, y, z, 1 - core)
    neighbour = device(x + 1 - 2 * xl, y, z, core)
    z_mate = device(x, y, z_at(toward), core)
    z1_up, z1_down = device(x, y, z_at(1), core), device(x, y, z_at(-1), core)
    z2_up, z2_down = device(x, y, z_at(2), core), device(x, y, z_at(-2), core)
    y_others = [(y + d) % 4 for d in (1, 3, 2)]
    y_up, y_down = device(x, y_others[0], z, core), device(x, y_others[1], z, core)
    near = [0, -toward, 2 * toward, -3 * toward]

    everyone = [z1_up, z1_down, z2_up, z2_down, device(x, y, z_at(-3 * toward), core)]
    everyone += [device(mirror, y, z_at(step), core) for step in near + [-2 * toward]]
    everyone += [device(x, y_, z, core) for y_ in y_others]
    everyone += [other_core, neighbour]
    barrier = pltpu.get_barrier_semaphore()
    for peer in everyone:
        pl.semaphore_signal(barrier, inc=1, device_id=peer, device_id_type=MESH)

    sent = []

    def send(src, dst, send_sem, recv_sem, peer):
        copy = pltpu.make_async_remote_copy(
            src_ref=src, dst_ref=dst, send_sem=send_sem, recv_sem=recv_sem,
            device_id=peer, device_id_type=MESH,
        )
        copy.start()
        return copy

    def wait_bytes(ref, sem):
        pltpu.make_async_copy(ref, ref, sem).wait()

    for load in loads:
        load.wait()

    def pick(idx_ref, table):
        slots = lax.broadcasted_iota(jnp.int32, table.shape, 0) * table.shape[1]
        slots += lax.broadcasted_iota(jnp.int32, table.shape, 1)
        rows = [
            jnp.sum(jnp.where(slots == idx_ref[i], table, 0.0), axis=0, keepdims=True)
            for i in range(PAIRS_HERE)
        ]
        return jnp.sum(jnp.concatenate(rows, axis=0), axis=1, keepdims=True)

    weight = 4.0 / (pick(val_ref, ve_ref[...]) - pick(cond_ref, ce_ref[...]))
    for j in range(0, e_ref.shape[1], HALF):
        part = e_ref[:, j : j + HALF].astype(F32)
        es[:, j : j + HALF] = (weight * part).astype(BF16)

    pl.semaphore_wait(barrier, len(everyone))

    own = zl + 3

    def send_b(g):
        for j in range(g * GROUP, g * GROUP + GROUP):

            def cols(y_, zl_):
                start = (y_ * 2 + zl_) * WIDE + j * CHUNK
                return pl.ds(pl.multiple_of(start, CHUNK), CHUNK)

            for y_ in y_others:
                for zl_, dst in ((zl, bp.at[j, own, xh, y]), (1 - zl, xs.at[j, y])):
                    send(
                        e_ref.at[:, cols(y_, zl_)], dst, a2a_s.at[2 + g], a2a_r.at[2 + g],
                        device(x, y_, z, core),
                    )
            bp[j, own, xh, y] = e_ref[:, cols(y, zl)]
            xs[j, y] = e_ref[:, cols(y, 1 - zl)]

    def wait_b(g):
        wait_bytes(bp.at[0, pl.ds(0, 3 * GROUP), 0, pl.ds(0, 2)], a2a_r.at[2 + g])

    def send_a(h):
        for step in near:
            z_ = z_at(step)
            place = (z - z_ // 2 * 2 + 11) % 8
            deep = pl.ds(place % 4 * 2 + xh, 1)
            for x_ in (x, mirror):
                part = 1 - x_ % 2 if h == 0 else x_ % 2
                start = (z_ // 2 * 2 + x_ // 2) * WIDE + part * HALF
                cols = pl.ds(pl.multiple_of(start, CHUNK), HALF)
                if x_ is x and step is near[0]:
                    a_in[h, place % 4 * 2 + xh] = es[:, cols]
                else:
                    send(
                        es.at[:, cols], a_in.at[h, place % 4 * 2 + xh],
                        a2a_s.at[h], a2a_r.at[h], device(x_, y, z_, core),
                    )

    def wait_a(h):
        wait_bytes(a_in.at[h, pl.ds(0, 7)], a2a_r.at[h])

    mate = y * 2 + 1 - zl
    up2, down2 = y_others[0] * 2, y_others[1] * 2

    def ag(h, n, slot, peer, rows=None):
        ref = at.at[h, slot] if rows is None else at.at[h, slot, pl.ds(*rows)]
        copy = send(ref, ref, ag_s.at[h, n], ag_r.at[h, n], peer)
        sent.append(copy)
        return copy

    def a_first(h):
        wait_a(h)
        at[h, col] = a_in[h].reshape(8 * PAIRS_HERE, HALF).T
        return [ag(h, 0, col, z_mate), ag(h, 1, col, y_up), ag(h, 2, col, y_down)]

    def a_second(h, first):
        first[0].wait_recv()
        return [ag(h, 3, mate, y_up), ag(h, 4, mate, y_down)]

    lo, hi = (0, QUARTER), (QUARTER, QUARTER)

    def a_third(h, first):
        first[1].wait_recv()
        one = ag(h, 5, down2 + zl, y_up, lo)
        first[2].wait_recv()
        return [one, ag(h, 6, up2 + zl, y_down, hi)]

    def a_fourth(h, second):
        second[0].wait_recv()
        one = ag(h, 7, down2 + 1 - zl, y_up, lo)
        second[1].wait_recv()
        return [one, ag(h, 8, up2 + 1 - zl, y_down, hi)]

    def a_last(copies):
        for copy in copies:
            copy.wait_recv()

    def bg(j, n, here, there, peer, rows=None):
        src, dst = (xs.at[j] if here is None else bp.at[j, here, xh]), bp.at[j, there, xh]
        if rows is not None:
            src, dst = src.at[pl.ds(*rows)], dst.at[pl.ds(*rows)]
        return send(src, dst, bg_s.at[j], bg_r.at[j, n], peer)

    def place_up(place, steps):
        return (place - 2 * steps + 8) % 8

    from_2d, from_2u, from_1d, from_1u, from_4, from_3d, from_3u = (
        (own + step + 8) % 8 for step in (-2, 2, -1, 1, 4, -3, 3)
    )

    chunks = [dict() for _ in range(CHUNKS)]

    def b_z(j):
        d = chunks[j]
        d["1u"] = bg(j, 0, None, place_up(own, zl), z1_up)
        d["1d"] = bg(j, 1, None, place_up(own, zl - 1), z1_down)
        d["2u"] = bg(j, 2, own, place_up(own, 1), z2_up)
        d["2d"] = bg(j, 3, own, place_up(own, -1), z2_down)

    def b_x(j, place=own):
        chunks[j]["m"] = bg(j, 8, place, place, mirror_dev)

    def b_second(j):
        d = chunks[j]
        d["1u"].wait_recv()
        d["3u"] = bg(j, 4, from_1d, place_up(from_1d, 1), z2_up)
        b_x(j, from_1d)
        d["1d"].wait_recv()
        d["3d"] = bg(j, 5, from_1u, place_up(from_1u, -1), z2_down)
        b_x(j, from_1u)
        d["2u"].wait_recv()
        d["4u"] = bg(j, 6, from_2d, place_up(from_2d, 1), z2_up, (0, 2))
        b_x(j, from_2d)
        d["2d"].wait_recv()
        d["4d"] = bg(j, 7, from_2u, place_up(from_2u, -1), z2_down, (2, 2))
        b_x(j, from_2u)

    def b_third(j):
        d = chunks[j]
        d["3u"].wait_recv()
        b_x(j, from_3d)
        d["3d"].wait_recv()
        b_x(j, from_3u)
        d["4u"].wait_recv()
        d["4d"].wait_recv()
        b_x(j, from_4)

    def b_last(j):
        wait_bytes(bp.at[j, :, 0], bg_r.at[j, 8])

    mine = pl.ds(pl.multiple_of(core * QUARTER, QUARTER), QUARTER)
    others = pl.ds(pl.multiple_of((1 - core) * QUARTER, QUARTER), QUARTER)

    def multiply(j, h):
        left = jnp.concatenate([at[h, n] for n in range(8)], axis=1)
        right = [
            bp[j, n % 2 * 4 : n % 2 * 4 + 4, :, n // 2].reshape(128, CHUNK) for n in range(8)
        ]
        right = jnp.concatenate(right, axis=0)
        c_own[j, h] = jnp.dot(left, right, preferred_element_type=F32)
        copy = send(c_own.at[j, h, others], c_got.at[j, h], c_s.at[j, h], c_r.at[j, h], other_core)
        sent.append(copy)
        chunks[j][f"c{h}"] = copy

    def give(j):
        chunks[j]["c0"].wait_recv()
        p_give[j] = (c_own[j, 0, mine] + c_got[j, 0]).astype(BF16)
        copy = send(p_give.at[j], p_got.at[j], p_s.at[j], p_r.at[j], neighbour)
        sent.append(copy)
        chunks[j]["p"] = copy

    eye = lax.broadcasted_iota(jnp.int32, (128, 128), 0) == lax.broadcasted_iota(
        jnp.int32, (128, 128), 1
    )
    row_scale = []
    for i in range(QUARTER // 128):
        line = cs_ref[:, pl.ds(pl.multiple_of(row * QUARTER + i * 128, 128), 128)]
        row_scale.append(jnp.sum(jnp.where(eye, line, 0.0), axis=1, keepdims=True))
    row_scale = jnp.concatenate(row_scale, axis=0)

    def finish(j):
        chunks[j]["c1"].wait_recv()
        chunks[j]["p"].wait_recv()
        total = c_own[j, 1, mine] + c_got[j, 1] + p_got[j].astype(F32)
        start = pl.multiple_of(col * WIDE + j * CHUNK, CHUNK)
        col_scale = cs_ref[:, pl.ds(start, CHUNK)]
        out_ref[:, j * CHUNK : (j + 1) * CHUNK] = row_scale * total * col_scale

    outs = []
    send_b(0)
    send_a(0)
    send_b(1)
    send_b(2)
    wait_b(0)
    b_z(0)
    b_x(0)
    b_x(1)
    b_z(1)
    wait_b(1)
    b_x(2)
    b_x(3)
    t1 = a_first(0)
    wait_b(2)
    b_x(4)
    b_x(5)
    b_second(0)
    b_second(1)
    b_z(2)
    t2 = a_second(0, t1)
    t3 = a_third(0, t1)
    b_z(3)
    b_third(0)
    b_third(1)
    send_a(1)
    t4 = a_fourth(0, t2)
    b_second(2)
    b_z(4)
    b_second(3)
    a_last(t3 + t4)
    b_last(0)
    multiply(0, 0)
    b_z(5)
    u1 = a_first(1)
    give(0)
    b_third(2)
    b_last(1)
    multiply(1, 0)
    b_third(3)
    give(1)
    b_second(4)
    u2 = a_second(1, u1)
    u3 = a_third(1, u1)
    b_second(5)
    b_last(2)
    multiply(2, 0)
    b_third(4)
    give(2)
    b_last(3)
    multiply(3, 0)
    b_third(5)
    u4 = a_fourth(1, u2)
    give(3)
    a_last(u3 + u4)
    multiply(0, 1)
    b_last(4)
    multiply(4, 0)
    multiply(1, 1)
    give(4)
    finish(0)
    multiply(2, 1)
    finish(1)
    b_last(5)
    multiply(5, 0)
    multiply(3, 1)
    give(5)
    finish(2)
    multiply(4, 1)
    finish(3)
    multiply(5, 1)
    finish(4)
    finish(5)

    for copy in outs:
        copy.wait()
    for copy in sent:
        copy.wait_send()
    for h in range(2):
        wait_bytes(a_in.at[h, pl.ds(0, 7)], a2a_s.at[h])
    for g in range(CHUNKS // GROUP):
        wait_bytes(bp.at[0, pl.ds(0, 3 * GROUP), 0, pl.ds(0, 2)], a2a_s.at[2 + g])
    for j in range(CHUNKS):
        wait_bytes(bp.at[pl.ds(0, 5), pl.ds(0, 3), 0], bg_s.at[j])


def per_device(
    pair_valence, pair_conduction, elements, valence_energy, conduction_energy, coulomb_sqrt
):
    n = CHUNKS
    dma = pltpu.SemaphoreType.DMA
    tables = (
        valence_energy.reshape(1, -1),
        conduction_energy.reshape(-1, 128),
        coulomb_sqrt.reshape(1, -1),
    )
    operands = [
        pltpu.with_memory_space_constraint(a, pltpu.HBM)
        for a in (pair_valence, pair_conduction, elements, *tables)
    ]
    return pl.pallas_call(
        kernel,
        out_shape=pltpu.VMEM((QUARTER, WIDE), F32),
        in_specs=[pl.BlockSpec(memory_space=pltpu.HBM)] * 6,
        out_specs=pl.BlockSpec(memory_space=pltpu.VMEM),
        scratch_shapes=[
            pltpu.SMEM((PAIRS_HERE,), jnp.int32),
            pltpu.SMEM((PAIRS_HERE,), jnp.int32),
            pltpu.VMEM(elements.shape, BF16),
            *(pltpu.VMEM(t.shape, F32) for t in tables),
            dma((6,)),
            pltpu.VMEM(elements.shape, BF16),
            pltpu.VMEM((2, 8, PAIRS_HERE, HALF), BF16),
            pltpu.VMEM((2, 8, HALF, 128), BF16),
            pltpu.VMEM((n, 8, 2, 4, PAIRS_HERE, CHUNK), BF16),
            pltpu.VMEM((n, 4, PAIRS_HERE, CHUNK), BF16),
            pltpu.VMEM((n, 2, HALF, CHUNK), F32),
            pltpu.VMEM((n, 2, QUARTER, CHUNK), F32),
            pltpu.VMEM((n, QUARTER, CHUNK), BF16),
            pltpu.VMEM((n, QUARTER, CHUNK), BF16),
            dma((5,)), dma((5,)),
            dma((2, 9)), dma((2, 9)),
            dma((n,)), dma((n, 9)),
            dma((n, 2)), dma((n, 2)),
            dma((n,)), dma((n,)),
        ],
        compiler_params=pltpu.CompilerParams(
            collective_id=0, has_side_effects=True, vmem_limit_bytes=48 * 2**20
        ),
        cost_estimate=pl.CostEstimate(
            flops=2 * 1024 * WIDE * WIDE, bytes_accessed=3 * 2**20, transcendentals=0
        ),
    )(*operands)


def solution(mesh):
    placed = (P(("row", "col")), P(("row", "col")), P(("row", "col"), None), P(), P(), P())
    return jax.shard_map(
        per_device, mesh=mesh, in_specs=placed, out_specs=P("row", "col"), check_vma=False
    )
```

time: 89.2 us -> 76.4 us (0.86)
  Pallas kernels: 82.5 us -> 74.1 us
  local copies, waits for them, and re-layouts: 5.87 us -> 1.41 us
    pallas_call x1, Pallas kernels: 82.5 us -> 74.1 us  [per_device(): pl.pallas_call(kernel, out_shape=pltpu.VMEM((QUARTER, WIDE), F32), in_spe...]
    unnamed x13 -> x1, local copies, waits for them, and re-layouts: 5.87 us -> 1.41 us
where the time goes in v2:
time: 76.4 us; the launch traced here: 75.6 us
  Pallas kernels  74.1 us (97%)
  local copies, waits for them, and re-layouts  1.41 us (2%)
    pallas_call x1, Pallas kernels, per_device(): pl.pallas_call(kernel, out_shape=pltpu.VMEM((QUARTER, WIDE), F32), in_spe...  74.1 us

profile of v2, /device:TPU:3, one launch (start us, length us, event | category | flops | bytes accessed | tf_op | source)
XLA Modules:
  0.0 75.6 jit_solution(3152044401328165464)
XLA Ops:
  0.0 74.1 %shard_map.64 = f32[384,1536]{1,0:T(8,128)S(1)} custom-call(s32[16]{0:T(128)} %val_hbm.1, s32[16]{0:T(128)} %cond_hbm.1, bf16[16,12288]{1,0:T(8,128)(2,1)} %e_hbm.1, f32[1,64]{1,0:T(1,128)} %bitcast.5, f32[24,128]{1,0:T(8,128)} %bitcast.4, f32[1,12288]{1,0:T(1,128)} %bitcast.3), custom_call_target="tpu_custom_call" | custom-call | flops 4831838208 | bytes 3145728 | tf_op jit(solution)/shard_map/pallas_call | solution.py:369
  74.2 1.4 %copy.8 = f32[384,1536]{1,0:T(8,128)} copy(f32[384,1536]{1,0:T(8,128)S(1)} %shard_map.64) | data formatting | bytes 4718592

commit v3 on v2

v3 whole, which is shorter than its diff:
```python
import jax
import jax.numpy as jnp
from jax import lax
from jax.experimental import pallas as pl
from jax.experimental.pallas import tpu as pltpu
from jax.sharding import PartitionSpec as P

MESH = pl.DeviceIdType.MESH
F32, BF16 = jnp.float32, jnp.bfloat16

PAIRS_HERE = 16
WIDE = 1536
HALF = WIDE // 2
QUARTER = WIDE // 4
CHUNKS = ((0, 256), (256, 256), (512, 256), (768, 256), (1024, 256), (1280, 128), (1408, 128))
GROUPS = ((0, 1), (2, 3), (4, 5, 6))
GROUP_WIDE = 512


def kernel(
    val_hbm, cond_hbm, e_hbm, ve_hbm, ce_hbm, cs_hbm, out_ref,
    val_ref, cond_ref, e_ref, ve_ref, ce_ref, cs_ref, in_s,
    es, a_in, at, bp, xs, c_give, c_got, p_give, p_got, d_own, d_got,
    a2a_s, a2a_r, ag_s, ag_r, bg_s, bg_r, c_s, c_r, d_s, d_r, p_s, p_r,
):
    loads = [
        pltpu.make_async_copy(far, near, in_s.at[i])
        for i, (far, near) in enumerate(
            (
                (e_hbm, e_ref), (val_hbm, val_ref), (cond_hbm, cond_ref),
                (ve_hbm, ve_ref), (ce_hbm, ce_ref), (cs_hbm, cs_ref),
            )
        )
    ]
    for load in loads:
        load.start()

    row, col = lax.axis_index("row"), lax.axis_index("col")
    core, x, zh = row % 2, (row // 2) % 4, row // 8
    y, zl = col // 2, col % 2
    xh, xl, z = x // 2, x % 2, zh * 2 + zl
    toward = 1 - 2 * zl

    def device(x_, y_, z_, core_):
        return ((z_ // 2 * 4 + x_) * 2 + core_, y_ * 2 + z_ % 2)

    def z_at(step):
        return (z + step + 8) % 8

    mirror = 3 - x
    mirror_dev = device(mirror, y, z, core)
    other_core = device(x, y, z, 1 - core)
    neighbour = device(x + 1 - 2 * xl, y, z, core)
    z_mate = device(x, y, z_at(toward), core)
    z1_up, z1_down = device(x, y, z_at(1), core), device(x, y, z_at(-1), core)
    z2_up, z2_down = device(x, y, z_at(2), core), device(x, y, z_at(-2), core)
    y_others = [(y + d) % 4 for d in (1, 3, 2)]
    y_up, y_down = device(x, y_others[0], z, core), device(x, y_others[1], z, core)
    near = [0, -toward, 2 * toward, -3 * toward]

    everyone = [z1_up, z1_down, z2_up, z2_down, device(x, y, z_at(-3 * toward), core)]
    everyone += [device(mirror, y, z_at(step), core) for step in near + [-2 * toward]]
    everyone += [device(x, y_, z, core) for y_ in y_others]
    everyone += [other_core, neighbour]
    barrier = pltpu.get_barrier_semaphore()
    for peer in everyone:
        pl.semaphore_signal(barrier, inc=1, device_id=peer, device_id_type=MESH)

    sent = []

    def send(src, dst, send_sem, recv_sem, peer):
        copy = pltpu.make_async_remote_copy(
            src_ref=src, dst_ref=dst, send_sem=send_sem, recv_sem=recv_sem,
            device_id=peer, device_id_type=MESH,
        )
        copy.start()
        return copy

    def wait_bytes(ref, sem):
        pltpu.make_async_copy(ref, ref, sem).wait()

    loads[0].wait()
    pl.semaphore_wait(barrier, len(everyone))

    own = zl + 3

    def send_b(g):
        for j in GROUPS[g]:
            first, wide = CHUNKS[j]

            def cols(y_, zl_):
                start = (y_ * 2 + zl_) * WIDE + first
                return pl.ds(pl.multiple_of(start, 128), wide)

            for y_ in y_others:
                for zl_, dst in ((zl, bp[j].at[own, xh, y]), (1 - zl, xs[j].at[y])):
                    send(
                        e_ref.at[:, cols(y_, zl_)], dst, a2a_s.at[2 + g], a2a_r.at[2 + g],
                        device(x, y_, z, core),
                    )
            bp[j][own, xh, y] = e_ref[:, cols(y, zl)]
            xs[j][y] = e_ref[:, cols(y, 1 - zl)]

    def wait_group(sem):
        wait_bytes(es.at[:, pl.ds(0, 3 * 2 * GROUP_WIDE)], sem)

    def wait_b(g):
        wait_group(a2a_r.at[2 + g])

    for g in range(len(GROUPS)):
        send_b(g)

    for load in loads[1:]:
        load.wait()

    def pick(idx_ref, table):
        slots = lax.broadcasted_iota(jnp.int32, table.shape, 0) * table.shape[1]
        slots += lax.broadcasted_iota(jnp.int32, table.shape, 1)
        rows = [
            jnp.sum(jnp.where(slots == idx_ref[i], table, 0.0), axis=0, keepdims=True)
            for i in range(PAIRS_HERE)
        ]
        return jnp.sum(jnp.concatenate(rows, axis=0), axis=1, keepdims=True)

    weight = 4.0 / (pick(val_ref, ve_ref[...]) - pick(cond_ref, ce_ref[...]))
    for j in range(0, e_ref.shape[1], HALF):
        part = e_ref[:, j : j + HALF].astype(F32)
        es[:, j : j + HALF] = (weight * part).astype(BF16)

    def send_a(h):
        for step in near[::-1]:
            z_ = z_at(step)
            place = (z - z_ // 2 * 2 + 11) % 8
            deep = pl.ds(place % 4 * 2 + xh, 1)
            for x_ in (mirror, x):
                part = 1 - x_ % 2 if h == 0 else x_ % 2
                start = (z_ // 2 * 2 + x_ // 2) * WIDE + part * HALF
                cols = pl.ds(pl.multiple_of(start, HALF), HALF)
                if x_ is x and step is near[0]:
                    a_in[h, place % 4 * 2 + xh] = es[:, cols]
                else:
                    send(
                        es.at[:, cols], a_in.at[h, place % 4 * 2 + xh],
                        a2a_s.at[h], a2a_r.at[h], device(x_, y, z_, core),
                    )

    def wait_a(h):
        wait_bytes(a_in.at[h, pl.ds(0, 7)], a2a_r.at[h])

    mate = y * 2 + 1 - zl
    up2, down2 = y_others[0] * 2, y_others[1] * 2

    def ag(h, n, slot, peer, rows=None):
        ref = at.at[h, slot] if rows is None else at.at[h, slot, pl.ds(*rows)]
        copy = send(ref, ref, ag_s.at[h, n], ag_r.at[h, n], peer)
        sent.append(copy)
        return copy

    halves = [dict(), dict()]
    lo, hi = (0, QUARTER), (QUARTER, QUARTER)

    def a_first(h):
        wait_a(h)
        at[h, col] = a_in[h].reshape(8 * PAIRS_HERE, HALF).T
        halves[h].update(
            mate_lo=ag(h, 0, col, z_mate, lo), mate_hi=ag(h, 1, col, z_mate, hi),
            up=ag(h, 2, col, y_up), down=ag(h, 3, col, y_down),
        )

    def a_third(h):
        d = halves[h]
        d["up"].wait_recv()
        d["far0"] = ag(h, 4, down2 + zl, y_up, lo)
        d["down"].wait_recv()
        d["far1"] = ag(h, 5, up2 + zl, y_down, hi)

    def a_second_lo(h):
        d = halves[h]
        d["mate_lo"].wait_recv()
        d.update(lo_up=ag(h, 6, mate, y_up, lo), lo_down=ag(h, 7, mate, y_down, lo))

    def a_second_hi(h):
        d = halves[h]
        d["mate_hi"].wait_recv()
        d.update(hi_up=ag(h, 8, mate, y_up, hi), hi_down=ag(h, 9, mate, y_down, hi))

    def a_fourth_lo(h):
        halves[h]["lo_up"].wait_recv()
        halves[h]["far2"] = ag(h, 10, down2 + 1 - zl, y_up, lo)

    def a_fourth_hi(h):
        halves[h]["hi_down"].wait_recv()
        halves[h]["far3"] = ag(h, 11, up2 + 1 - zl, y_down, hi)

    def a_last(h):
        for name in ("lo_down", "hi_up", "far0", "far1", "far2", "far3"):
            halves[h][name].wait_recv()

    def place_at(source, reader):
        there = z_at(reader * toward) // 2
        return (z + source * toward - 2 * there + 19) % 8

    def bg(j, n, source, step, rows=None):
        src = xs[j] if step in (1, -1) else bp[j].at[place_at(source, 0), xh]
        dst = bp[j].at[place_at(source, step), xh]
        if rows is not None:
            src, dst = src.at[pl.ds(*rows)], dst.at[pl.ds(*rows)]
        peer = device(x, y, z_at(step * toward), core)
        return send(src, dst, bg_s.at[j], bg_r.at[j, n], peer)

    chunks = [dict() for _ in CHUNKS]

    def b_z(j):
        chunks[j]["1t"] = bg(j, 0, 0, 1)
        chunks[j]["1a"] = bg(j, 1, 0, -1)
        chunks[j]["2t"] = bg(j, 2, 0, 2)
        chunks[j]["2a"] = bg(j, 3, 0, -2)

    def b_x(j, source=0):
        block = bp[j].at[place_at(source, 0), xh]
        send(block, block, bg_s.at[j], bg_r.at[j, 8], mirror_dev)

    def b_1t(j):
        chunks[j]["1t"].wait_recv()
        chunks[j]["3a"] = bg(j, 4, 1, -2)
        b_x(j, 1)

    def b_1a(j):
        chunks[j]["1a"].wait_recv()
        chunks[j]["3t"] = bg(j, 5, -1, 2)
        b_x(j, -1)

    def b_2t(j):
        chunks[j]["2t"].wait_recv()
        chunks[j]["4t"] = bg(j, 6, -2, 2, (0, 2))
        b_x(j, -2)

    def b_2a(j):
        chunks[j]["2a"].wait_recv()
        chunks[j]["4a"] = bg(j, 7, 2, -2, (2, 2))
        b_x(j, 2)

    def b_3t(j):
        chunks[j]["3t"].wait_recv()
        b_x(j, -3)

    def b_3a(j):
        chunks[j]["3a"].wait_recv()
        b_x(j, 3)

    def b_4(j):
        chunks[j]["4t"].wait_recv()
        chunks[j]["4a"].wait_recv()
        b_x(j, 4)

    def b_last(j):
        wait_bytes(bp[j].at[:, 0], bg_r.at[j, 8])

    def rows_of(q):
        return pl.ds(pl.multiple_of(q * QUARTER, QUARTER), QUARTER)

    def columns(j):
        wide = CHUNKS[j][1]
        parts = [bp[j][n % 2 * 4 : n % 2 * 4 + 4, :, n // 2].reshape(128, wide) for n in range(8)]
        return jnp.concatenate(parts, axis=0)

    def product(h, right, out, got, send_sem, recv_sem):
        @pl.loop(0, 2)
        def _(i):
            rows = rows_of((1 - core + i) % 2)
            left = jnp.concatenate([at[h, n, rows] for n in range(8)], axis=1)
            out[rows] = jnp.dot(left, right, preferred_element_type=F32)

            @pl.when(i == 0)
            def _():
                send(out.at[rows], got, send_sem, recv_sem, other_core)

    def multiply(j):
        product(0, columns(j), c_give[j], c_got[j], c_s.at[j], c_r.at[j])

    def multiply_own(g):
        right = jnp.concatenate([columns(j) for j in GROUPS[g]], axis=1)
        product(1, right, d_own.at[g], d_got.at[g], d_s.at[g], d_r.at[g])

    def give(j):
        wait_bytes(c_got[j], c_r.at[j])
        p_give[j][...] = (c_give[j][rows_of(core)] + c_got[j][...]).astype(BF16)
        sent.append(send(p_give[j], p_got[j], p_s.at[j], p_r.at[j], neighbour))

    eye = lax.broadcasted_iota(jnp.int32, (128, 128), 0) == lax.broadcasted_iota(
        jnp.int32, (128, 128), 1
    )
    row_scale = []
    for i in range(QUARTER // 128):
        line = cs_ref[:, pl.ds(pl.multiple_of(row * QUARTER + i * 128, 128), 128)]
        row_scale.append(jnp.sum(jnp.where(eye, line, 0.0), axis=1, keepdims=True))
    row_scale = jnp.concatenate(row_scale, axis=0)

    def finish_own(g):
        wait_bytes(d_got.at[g], d_r.at[g])
        d_got[g] += d_own[g, rows_of(core)]

    def finish(j):
        wait_bytes(p_got[j], p_r.at[j])
        first, wide = CHUNKS[j]
        in_group = pl.ds(first % GROUP_WIDE, wide)
        total = d_got[first // GROUP_WIDE, :, in_group] + p_got[j][...].astype(F32)
        start = pl.multiple_of(col * WIDE + first, 128)
        col_scale = cs_ref[:, pl.ds(start, wide)]
        out_ref[:, first : first + wide] = row_scale * total * col_scale

    outs = []
    send_a(0)
    wait_b(0)
    b_z(0)
    b_x(0)
    b_x(1)
    b_z(1)
    wait_b(1)
    b_x(2)
    b_x(3)
    a_first(0)
    wait_b(2)
    b_x(4)
    b_x(5)
    b_x(6)
    b_1t(0)
    b_1a(0)
    b_2t(0)
    b_2a(0)
    b_1t(1)
    b_1a(1)
    b_2t(1)
    b_2a(1)
    b_z(2)
    a_third(0)
    a_second_lo(0)
    b_z(3)
    a_second_hi(0)
    send_a(1)
    b_3t(0)
    b_3a(0)
    b_4(0)
    b_3t(1)
    b_3a(1)
    b_4(1)
    a_fourth_lo(0)
    b_1t(2)
    b_1a(2)
    b_2t(2)
    b_2a(2)
    b_z(4)
    a_fourth_hi(0)
    b_1t(3)
    b_1a(3)
    b_2t(3)
    b_2a(3)
    b_z(5)
    b_z(6)
    a_last(0)
    b_last(0)
    multiply(0)
    a_first(1)
    b_3t(2)
    b_3a(2)
    b_4(2)
    give(0)
    b_last(1)
    multiply(1)
    b_3t(3)
    b_3a(3)
    b_4(3)
    b_1t(4)
    b_1a(4)
    b_2t(4)
    b_2a(4)
    give(1)
    b_last(2)
    multiply(2)
    a_third(1)
    a_second_lo(1)
    b_1t(5)
    b_1a(5)
    b_2t(5)
    b_2a(5)
    a_second_hi(1)
    give(2)
    b_1t(6)
    b_1a(6)
    b_2t(6)
    b_2a(6)
    b_3t(4)
    b_3a(4)
    b_4(4)
    b_last(3)
    multiply(3)
    b_3t(5)
    b_3a(5)
    b_4(5)
    a_fourth_lo(1)
    b_3t(6)
    b_3a(6)
    b_4(6)
    give(3)
    a_fourth_hi(1)
    b_last(4)
    multiply(4)
    b_last(5)
    give(4)
    multiply(5)
    b_last(6)
    multiply(6)
    give(5)
    a_last(1)
    give(6)
    multiply_own(0)
    multiply_own(1)
    multiply_own(2)
    finish_own(0)
    finish(0)
    finish(1)
    finish_own(1)
    finish(2)
    finish(3)
    finish_own(2)
    finish(4)
    finish(5)
    finish(6)

    for copy in outs:
        copy.wait()
    for copy in sent:
        copy.wait_send()
    for h in range(2):
        wait_bytes(a_in.at[h, pl.ds(0, 7)], a2a_s.at[h])
    for g in range(len(GROUPS)):
        wait_group(a2a_s.at[2 + g])
        wait_bytes(d_got.at[g], d_s.at[g])
    for j, (_, wide) in enumerate(CHUNKS):
        wait_bytes(c_got[j], c_s.at[j])
        wait_bytes(at.at[0, pl.ds(0, 5), pl.ds(0, 12 * wide // 8)], bg_s.at[j])


def per_device(
    pair_valence, pair_conduction, elements, valence_energy, conduction_energy, coulomb_sqrt
):
    n = len(CHUNKS)

    def each(*shape, dtype=BF16):
        return [pltpu.VMEM((*shape, wide), dtype) for _, wide in CHUNKS]

    dma = pltpu.SemaphoreType.DMA
    tables = (
        valence_energy.reshape(1, -1),
        conduction_energy.reshape(-1, 128),
        coulomb_sqrt.reshape(1, -1),
    )
    operands = [
        pltpu.with_memory_space_constraint(a, pltpu.HBM)
        for a in (pair_valence, pair_conduction, elements, *tables)
    ]
    return pl.pallas_call(
        kernel,
        out_shape=pltpu.VMEM((QUARTER, WIDE), F32),
        in_specs=[pl.BlockSpec(memory_space=pltpu.HBM)] * 6,
        out_specs=pl.BlockSpec(memory_space=pltpu.VMEM),
        scratch_shapes=[
            pltpu.SMEM((PAIRS_HERE,), jnp.int32),
            pltpu.SMEM((PAIRS_HERE,), jnp.int32),
            pltpu.VMEM(elements.shape, BF16),
            *(pltpu.VMEM(t.shape, F32) for t in tables),
            dma((6,)),
            pltpu.VMEM(elements.shape, BF16),
            pltpu.VMEM((2, 8, PAIRS_HERE, HALF), BF16),
            pltpu.VMEM((2, 8, HALF, 128), BF16),
            each(8, 2, 4, PAIRS_HERE),
            each(4, PAIRS_HERE),
            each(HALF, dtype=F32),
            each(QUARTER, dtype=F32),
            each(QUARTER),
            each(QUARTER),
            pltpu.VMEM((len(GROUPS), HALF, GROUP_WIDE), F32),
            pltpu.VMEM((len(GROUPS), QUARTER, GROUP_WIDE), F32),
            dma((5,)), dma((5,)),
            dma((2, 12)), dma((2, 12)),
            dma((n,)), dma((n, 9)),
            dma((n,)), dma((n,)),
            dma((len(GROUPS),)), dma((len(GROUPS),)),
            dma((n,)), dma((n,)),
        ],
        compiler_params=pltpu.CompilerParams(
            collective_id=0, has_side_effects=True, vmem_limit_bytes=48 * 2**20
        ),
        cost_estimate=pl.CostEstimate(
            flops=2 * 1024 * WIDE * WIDE, bytes_accessed=3 * 2**20, transcendentals=0
        ),
    )(*operands)


def solution(mesh):
    placed = (P(("row", "col")), P(("row", "col")), P(("row", "col"), None), P(), P(), P())
    return jax.shard_map(
        per_device, mesh=mesh, in_specs=placed, out_specs=P("row", "col"), check_vma=False
    )
```

time: 76.4 us -> 70.2 us (0.919)
  Pallas kernels: 74.1 us -> 68.1 us
    pallas_call x1, Pallas kernels: 74.1 us -> 68.1 us  [per_device(): pl.pallas_call(kernel, out_shape=pltpu.VMEM((QUARTER, WIDE), F32), in_spe...]
where the time goes in v3:
time: 70.2 us; the launch traced here: 69.5 us
  Pallas kernels  68.1 us (97%)
  local copies, waits for them, and re-layouts  1.41 us (2%)
    pallas_call x1, Pallas kernels, per_device(): pl.pallas_call(kernel, out_shape=pltpu.VMEM((QUARTER, WIDE), F32), in_spe...  68.1 us
    unnamed x1, local copies, waits for them, and re-layouts  1.41 us

profile of v3, /device:TPU:3, one launch (start us, length us, event | category | flops | bytes accessed | tf_op | source)
XLA Modules:
  0.0 69.5 jit_solution(10764671894926948299)
XLA Ops:
  0.0 68.1 %shard_map.64 = f32[384,1536]{1,0:T(8,128)S(1)} custom-call(s32[16]{0:T(128)} %val_hbm.1, s32[16]{0:T(128)} %cond_hbm.1, bf16[16,12288]{1,0:T(8,128)(2,1)} %e_hbm.1, f32[1,64]{1,0:T(1,128)} %bitcast.5, f32[24,128]{1,0:T(8,128)} %bitcast.4, f32[1,12288]{1,0:T(1,128)} %bitcast.3), custom_call_target="tpu_custom_call" | custom-call | flops 4831838208 | bytes 3145728 | tf_op jit(solution)/shard_map/pallas_call | solution.py:462
  68.1 1.4 %copy.8 = f32[384,1536]{1,0:T(8,128)} copy(f32[384,1536]{1,0:T(8,128)S(1)} %shard_map.64) | data formatting | bytes 4718592

commit v4 on v3

--- a/solution.py
+++ b/solution.py
@@ -12,8 +12,8 @@
 WIDE = 1536
 HALF = WIDE // 2
 QUARTER = WIDE // 4
-CHUNKS = ((0, 256), (256, 256), (512, 256), (768, 256), (1024, 256), (1280, 128), (1408, 128))
-GROUPS = ((0, 1), (2, 3), (4, 5, 6))
+CHUNKS = ((0, 256), (256, 256), (512, 256), (768, 256), (1024, 128), (1152, 128), (1280, 128), (1408, 128))
+GROUPS = ((0, 1), (2, 3), (4, 5, 6, 7))
 GROUP_WIDE = 512
 
 
@@ -21,7 +21,7 @@
     val_hbm, cond_hbm, e_hbm, ve_hbm, ce_hbm, cs_hbm, out_ref,
     val_ref, cond_ref, e_ref, ve_ref, ce_ref, cs_ref, in_s,
     es, a_in, at, bp, xs, c_give, c_got, p_give, p_got, d_own, d_got,
-    a2a_s, a2a_r, ag_s, ag_r, bg_s, bg_r, c_s, c_r, d_s, d_r, p_s, p_r,
+    a2a_s, a2a_r, ag_s, ag_r, bg_s, bg_r, c_s, c_r, d_r, p_s, p_r,
 ):
     loads = [
         pltpu.make_async_copy(far, near, in_s.at[i])
@@ -66,8 +66,6 @@
     for peer in everyone:
         pl.semaphore_signal(barrier, inc=1, device_id=peer, device_id_type=MESH)
 
-    sent = []
-
     def send(src, dst, send_sem, recv_sem, peer):
         copy = pltpu.make_async_remote_copy(
             src_ref=src, dst_ref=dst, send_sem=send_sem, recv_sem=recv_sem,
@@ -95,7 +93,7 @@
             for y_ in y_others:
                 for zl_, dst in ((zl, bp[j].at[own, xh, y]), (1 - zl, xs[j].at[y])):
                     send(
-                        e_ref.at[:, cols(y_, zl_)], dst, a2a_s.at[2 + g], a2a_r.at[2 + g],
+                        e_ref.at[:, cols(y_, zl_)], dst, a2a_s, a2a_r.at[2 + g],
                         device(x, y_, z, core),
                     )
             bp[j][own, xh, y] = e_ref[:, cols(y, zl)]
@@ -141,7 +139,7 @@
                 else:
                     send(
                         es.at[:, cols], a_in.at[h, place % 4 * 2 + xh],
-                        a2a_s.at[h], a2a_r.at[h], device(x_, y, z_, core),
+                        a2a_s, a2a_r.at[h], device(x_, y, z_, core),
                     )
 
     def wait_a(h):
@@ -152,9 +150,7 @@
 
     def ag(h, n, slot, peer, rows=None):
         ref = at.at[h, slot] if rows is None else at.at[h, slot, pl.ds(*rows)]
-        copy = send(ref, ref, ag_s.at[h, n], ag_r.at[h, n], peer)
-        sent.append(copy)
-        return copy
+        return send(ref, ref, ag_s, ag_r.at[h, n], peer)
 
     halves = [dict(), dict()]
     lo, hi = (0, QUARTER), (QUARTER, QUARTER)
@@ -164,37 +160,37 @@
         at[h, col] = a_in[h].reshape(8 * PAIRS_HERE, HALF).T
         halves[h].update(
             mate_lo=ag(h, 0, col, z_mate, lo), mate_hi=ag(h, 1, col, z_mate, hi),
-            up=ag(h, 2, col, y_up), down=ag(h, 3, col, y_down),
         )
+        ag(h, 2, col, y_up)
+        ag(h, 2, col, y_down)
 
     def a_third(h):
-        d = halves[h]
-        d["up"].wait_recv()
-        d["far0"] = ag(h, 4, down2 + zl, y_up, lo)
-        d["down"].wait_recv()
-        d["far1"] = ag(h, 5, up2 + zl, y_down, hi)
+        wait_bytes(at.at[h, pl.ds(0, 2)], ag_r.at[h, 2])
+        ag(h, 3, down2 + zl, y_up, lo)
+        ag(h, 3, up2 + zl, y_down, hi)
 
     def a_second_lo(h):
         d = halves[h]
         d["mate_lo"].wait_recv()
-        d.update(lo_up=ag(h, 6, mate, y_up, lo), lo_down=ag(h, 7, mate, y_down, lo))
+        d["lo_up"] = ag(h, 4, mate, y_up, lo)
+        ag(h, 3, mate, y_down, lo)
 
     def a_second_hi(h):
         d = halves[h]
         d["mate_hi"].wait_recv()
-        d.update(hi_up=ag(h, 8, mate, y_up, hi), hi_down=ag(h, 9, mate, y_down, hi))
+        ag(h, 3, mate, y_up, hi)
+        d["hi_down"] = ag(h, 5, mate, y_down, hi)
 
     def a_fourth_lo(h):
         halves[h]["lo_up"].wait_recv()
-        halves[h]["far2"] = ag(h, 10, down2 + 1 - zl, y_up, lo)
+        ag(h, 3, down2 + 1 - zl, y_up, lo)
 
     def a_fourth_hi(h):
         halves[h]["hi_down"].wait_recv()
-        halves[h]["far3"] = ag(h, 11, up2 + 1 - zl, y_down, hi)
+        ag(h, 3, up2 + 1 - zl, y_down, hi)
 
     def a_last(h):
-        for name in ("lo_down", "hi_up", "far0", "far1", "far2", "far3"):
-            halves[h][name].wait_recv()
+        wait_bytes(at.at[h, pl.ds(0, 3)], ag_r.at[h, 3])
 
     def place_at(source, reader):
         there = z_at(reader * toward) // 2
@@ -206,55 +202,40 @@
         if rows is not None:
             src, dst = src.at[pl.ds(*rows)], dst.at[pl.ds(*rows)]
         peer = device(x, y, z_at(step * toward), core)
-        return send(src, dst, bg_s.at[j], bg_r.at[j, n], peer)
-
-    chunks = [dict() for _ in CHUNKS]
+        return send(src, dst, bg_s, bg_r.at[j, n], peer)
 
     def b_z(j):
-        chunks[j]["1t"] = bg(j, 0, 0, 1)
-        chunks[j]["1a"] = bg(j, 1, 0, -1)
-        chunks[j]["2t"] = bg(j, 2, 0, 2)
-        chunks[j]["2a"] = bg(j, 3, 0, -2)
+        bg(j, 0, 0, 1)
+        bg(j, 0, 0, -1)
+        bg(j, 1, 0, 2)
+        bg(j, 1, 0, -2)
 
     def b_x(j, source=0):
         block = bp[j].at[place_at(source, 0), xh]
-        send(block, block, bg_s.at[j], bg_r.at[j, 8], mirror_dev)
-
-    def b_1t(j):
-        chunks[j]["1t"].wait_recv()
-        chunks[j]["3a"] = bg(j, 4, 1, -2)
+        send(block, block, bg_s, bg_r.at[j, 3], mirror_dev)
+
+    def b_1(j):
+        wait_bytes(bp[j].at[pl.ds(0, 2), 0], bg_r.at[j, 0])
+        bg(j, 2, 1, -2)
         b_x(j, 1)
-
-    def b_1a(j):
-        chunks[j]["1a"].wait_recv()
-        chunks[j]["3t"] = bg(j, 5, -1, 2)
+        bg(j, 2, -1, 2)
         b_x(j, -1)
 
-    def b_2t(j):
-        chunks[j]["2t"].wait_recv()
-        chunks[j]["4t"] = bg(j, 6, -2, 2, (0, 2))
+    def b_2(j):
+        wait_bytes(bp[j].at[pl.ds(0, 2), 0], bg_r.at[j, 1])
+        bg(j, 2, -2, 2, (0, 2))
         b_x(j, -2)
-
-    def b_2a(j):
-        chunks[j]["2a"].wait_recv()
-        chunks[j]["4a"] = bg(j, 7, 2, -2, (2, 2))
+        bg(j, 2, 2, -2, (2, 2))
         b_x(j, 2)
 
-    def b_3t(j):
-        chunks[j]["3t"].wait_recv()
+    def b_3(j):
+        wait_bytes(bp[j].at[pl.ds(0, 3), 0], bg_r.at[j, 2])
         b_x(j, -3)
-
-    def b_3a(j):
-        chunks[j]["3a"].wait_recv()
         b_x(j, 3)
-
-    def b_4(j):
-        chunks[j]["4t"].wait_recv()
-        chunks[j]["4a"].wait_recv()
         b_x(j, 4)
 
     def b_last(j):
-        wait_bytes(bp[j].at[:, 0], bg_r.at[j, 8])
+        wait_bytes(bp[j].at[:, 0], bg_r.at[j, 3])
 
     def rows_of(q):
         return pl.ds(pl.multiple_of(q * QUARTER, QUARTER), QUARTER)
@@ -276,16 +257,16 @@
                 send(out.at[rows], got, send_sem, recv_sem, other_core)
 
     def multiply(j):
-        product(0, columns(j), c_give[j], c_got[j], c_s.at[j], c_r.at[j])
+        product(0, columns(j), c_give[j], c_got[j], c_s, c_r.at[j])
 
     def multiply_own(g):
         right = jnp.concatenate([columns(j) for j in GROUPS[g]], axis=1)
-        product(1, right, d_own.at[g], d_got.at[g], d_s.at[g], d_r.at[g])
+        product(1, right, d_own.at[g], d_got.at[g], c_s, d_r.at[g])
 
     def give(j):
         wait_bytes(c_got[j], c_r.at[j])
         p_give[j][...] = (c_give[j][rows_of(core)] + c_got[j][...]).astype(BF16)
-        sent.append(send(p_give[j], p_got[j], p_s.at[j], p_r.at[j], neighbour))
+        send(p_give[j], p_got[j], p_s, p_r.at[j], neighbour)
 
     eye = lax.broadcasted_iota(jnp.int32, (128, 128), 0) == lax.broadcasted_iota(
         jnp.int32, (128, 128), 1
@@ -324,83 +305,60 @@
     b_x(4)
     b_x(5)
     b_x(6)
-    b_1t(0)
-    b_1a(0)
-    b_2t(0)
-    b_2a(0)
-    b_1t(1)
-    b_1a(1)
-    b_2t(1)
-    b_2a(1)
+    b_x(7)
+    b_1(0)
+    b_2(0)
+    b_1(1)
+    b_2(1)
     b_z(2)
     a_third(0)
     a_second_lo(0)
     b_z(3)
     a_second_hi(0)
     send_a(1)
-    b_3t(0)
-    b_3a(0)
-    b_4(0)
-    b_3t(1)
-    b_3a(1)
-    b_4(1)
+    b_3(0)
+    b_3(1)
     a_fourth_lo(0)
-    b_1t(2)
-    b_1a(2)
-    b_2t(2)
-    b_2a(2)
+    b_1(2)
+    b_2(2)
     b_z(4)
     a_fourth_hi(0)
-    b_1t(3)
-    b_1a(3)
-    b_2t(3)
-    b_2a(3)
+    b_1(3)
+    b_2(3)
     b_z(5)
     b_z(6)
+    b_z(7)
     a_last(0)
     b_last(0)
     multiply(0)
     a_first(1)
-    b_3t(2)
-    b_3a(2)
-    b_4(2)
+    b_3(2)
     give(0)
     b_last(1)
     multiply(1)
-    b_3t(3)
-    b_3a(3)
-    b_4(3)
-    b_1t(4)
-    b_1a(4)
-    b_2t(4)
-    b_2a(4)
+    b_3(3)
+    b_1(4)
+    b_2(4)
     give(1)
     b_last(2)
     multiply(2)
     a_third(1)
     a_second_lo(1)
-    b_1t(5)
-    b_1a(5)
-    b_2t(5)
-    b_2a(5)
+    b_1(5)
+    b_2(5)
     a_second_hi(1)
     give(2)
-    b_1t(6)
-    b_1a(6)
-    b_2t(6)
-    b_2a(6)
-    b_3t(4)
-    b_3a(4)
-    b_4(4)
+    b_1(6)
+    b_1(7)
+    b_2(6)
+    b_2(7)
+    b_3(4)
     b_last(3)
     multiply(3)
-    b_3t(5)
-    b_3a(5)
-    b_4(5)
+    b_3(5)
     a_fourth_lo(1)
-    b_3t(6)
-    b_3a(6)
-    b_4(6)
+    b_3(6)
+    b_3(7)
     give(3)
     a_fourth_hi(1)
     b_last(4)
@@ -409,10 +367,13 @@
     give(4)
     multiply(5)
     b_last(6)
+    b_last(7)
     multiply(6)
+    multiply(7)
     give(5)
     a_last(1)
     give(6)
+    give(7)
     multiply_own(0)
     multiply_own(1)
     multiply_own(2)
@@ -426,19 +387,15 @@
     finish(4)
     finish(5)
     finish(6)
+    finish(7)
 
     for copy in outs:
         copy.wait()
-    for copy in sent:
-        copy.wait_send()
-    for h in range(2):
-        wait_bytes(a_in.at[h, pl.ds(0, 7)], a2a_s.at[h])
-    for g in range(len(GROUPS)):
-        wait_group(a2a_s.at[2 + g])
-        wait_bytes(d_got.at[g], d_s.at[g])
-    for j, (_, wide) in enumerate(CHUNKS):
-        wait_bytes(c_got[j], c_s.at[j])
-        wait_bytes(at.at[0, pl.ds(0, 5), pl.ds(0, 12 * wide // 8)], bg_s.at[j])
+    wait_bytes(at.at[0, pl.ds(0, 4), pl.ds(0, 624)], a2a_s)
+    wait_bytes(at.at[:, pl.ds(0, 7)], ag_s)
+    wait_bytes(at.at[:, :, pl.ds(0, 720)], bg_s)
+    wait_bytes(d_own, c_s)
+    wait_bytes(at.at[0, pl.ds(0, 6)], p_s)
 
 
 def per_device(
@@ -481,12 +438,12 @@
             each(QUARTER),
             pltpu.VMEM((len(GROUPS), HALF, GROUP_WIDE), F32),
             pltpu.VMEM((len(GROUPS), QUARTER, GROUP_WIDE), F32),
-            dma((5,)), dma((5,)),
-            dma((2, 12)), dma((2, 12)),
-            dma((n,)), dma((n, 9)),
-            dma((n,)), dma((n,)),
-            dma((len(GROUPS),)), dma((len(GROUPS),)),
-            dma((n,)), dma((n,)),
+            dma, dma((5,)),
+            dma, dma((2, 6)),
+            dma, dma((n, 4)),
+            dma, dma((n,)),
+            dma((len(GROUPS),)),
+            dma, dma((n,)),
         ],
         compiler_params=pltpu.CompilerParams(
             collective_id=0, has_side_effects=True, vmem_limit_bytes=48 * 2**20

time: 70.2 us -> 69 us (0.983)
  Pallas kernels: 68.1 us -> 67.3 us
    pallas_call x1, Pallas kernels: 68.1 us -> 67.3 us  [per_device(): pl.pallas_call(kernel, out_shape=pltpu.VMEM((QUARTER, WIDE), F32), in_spe...]
where the time goes in v4:
time: 69 us; the launch traced here: 68.7 us
  Pallas kernels  67.3 us (98%)
  local copies, waits for them, and re-layouts  1.41 us (2%)
    pallas_call x1, Pallas kernels, per_device(): pl.pallas_call(kernel, out_shape=pltpu.VMEM((QUARTER, WIDE), F32), in_spe...  67.3 us
    unnamed x1, local copies, waits for them, and re-layouts  1.41 us

profile of v4, /device:TPU:3, one launch (start us, length us, event | category | flops | bytes accessed | tf_op | source)
XLA Modules:
  0.0 68.7 jit_solution(15409301936110036197)
XLA Ops:
  0.0 67.3 %shard_map.64 = f32[384,1536]{1,0:T(8,128)S(1)} custom-call(s32[16]{0:T(128)} %val_hbm.1, s32[16]{0:T(128)} %cond_hbm.1, bf16[16,12288]{1,0:T(8,128)(2,1)} %e_hbm.1, f32[1,64]{1,0:T(1,128)} %bitcast.5, f32[24,128]{1,0:T(8,128)} %bitcast.4, f32[1,12288]{1,0:T(1,128)} %bitcast.3), custom_call_target="tpu_custom_call" | custom-call | flops 4831838208 | bytes 3145728 | tf_op jit(solution)/shard_map/pallas_call | solution.py:419
  67.3 1.4 %copy.8 = f32[384,1536]{1,0:T(8,128)} copy(f32[384,1536]{1,0:T(8,128)S(1)} %shard_map.64) | data formatting | bytes 4718592

commit v5 on v4

--- a/solution.py
+++ b/solution.py
@@ -78,6 +78,23 @@
         pltpu.make_async_copy(ref, ref, sem).wait()
 
     loads[0].wait()
+    for load in loads[1:]:
+        load.wait()
+
+    def pick(idx_ref, table):
+        slots = lax.broadcasted_iota(jnp.int32, table.shape, 0) * table.shape[1]
+        slots += lax.broadcasted_iota(jnp.int32, table.shape, 1)
+        rows = [
+            jnp.sum(jnp.where(slots == idx_ref[i], table, 0.0), axis=0, keepdims=True)
+            for i in range(PAIRS_HERE)
+        ]
+        return jnp.sum(jnp.concatenate(rows, axis=0), axis=1, keepdims=True)
+
+    weight = 4.0 / (pick(val_ref, ve_ref[...]) - pick(cond_ref, ce_ref[...]))
+    for j in range(0, e_ref.shape[1], HALF):
+        part = e_ref[:, j : j + HALF].astype(F32)
+        es[:, j : j + HALF] = (weight * part).astype(BF16)
+
     pl.semaphore_wait(barrier, len(everyone))
 
     own = zl + 3
@@ -107,23 +124,6 @@
 
     for g in range(len(GROUPS)):
         send_b(g)
-
-    for load in loads[1:]:
-        load.wait()
-
-    def pick(idx_ref, table):
-        slots = lax.broadcasted_iota(jnp.int32, table.shape, 0) * table.shape[1]
-        slots += lax.broadcasted_iota(jnp.int32, table.shape, 1)
-        rows = [
-            jnp.sum(jnp.where(slots == idx_ref[i], table, 0.0), axis=0, keepdims=True)
-            for i in range(PAIRS_HERE)
-        ]
-        return jnp.sum(jnp.concatenate(rows, axis=0), axis=1, keepdims=True)
-
-    weight = 4.0 / (pick(val_ref, ve_ref[...]) - pick(cond_ref, ce_ref[...]))
-    for j in range(0, e_ref.shape[1], HALF):
-        part = e_ref[:, j : j + HALF].astype(F32)
-        es[:, j : j + HALF] = (weight * part).astype(BF16)
 
     def send_a(h):
         for step in near[::-1]:

time: 69 us -> 69.1 us (level)
  no operation moved by 1% of the time
where the time goes in v5:
time: 69.1 us; the launch traced here: 68.6 us
  Pallas kernels  67.2 us (97%)
  local copies, waits for them, and re-layouts  1.41 us (2%)
    pallas_call x1, Pallas kernels, per_device(): pl.pallas_call(kernel, out_shape=pltpu.VMEM((QUARTER, WIDE), F32), in_spe...  67.2 us
    unnamed x1, local copies, waits for them, and re-layouts  1.41 us

profile of v5, /device:TPU:3, one launch (start us, length us, event | category | flops | bytes accessed | tf_op | source)
XLA Modules:
  0.0 68.6 jit_solution(14400416508787564070)
XLA Ops:
  0.0 67.2 %shard_map.64 = f32[384,1536]{1,0:T(8,128)S(1)} custom-call(s32[16]{0:T(128)} %val_hbm.1, s32[16]{0:T(128)} %cond_hbm.1, bf16[16,12288]{1,0:T(8,128)(2,1)} %e_hbm.1, f32[1,64]{1,0:T(1,128)} %bitcast.5, f32[24,128]{1,0:T(8,128)} %bitcast.4, f32[1,12288]{1,0:T(1,128)} %bitcast.3), custom_call_target="tpu_custom_call" | custom-call | flops 4831838208 | bytes 3145728 | tf_op jit(solution)/shard_map/pallas_call | solution.py:419
  67.2 1.4 %copy.8 = f32[384,1536]{1,0:T(8,128)} copy(f32[384,1536]{1,0:T(8,128)S(1)} %shard_map.64) | data formatting | bytes 4718592
